TPU v7x, 128 devices: a whole 4x4x4 slice. The times are simulated.
128 devices in a mesh: tm: 32 (over y, x, core), hid: 4 (over z).
Axes of the slice: x: 4, y: 4, z: 4, core: 2. Of those that a mesh axis runs over, the one named last changes fastest.
Arguments:
- gate_inputs: bfloat16 [8192, 3, 4096], P('tm', None, 'hid'), may hold values from -6 to 16
- recurrent: bfloat16 [3, 4096, 4096], P(None, None, 'hid'), may hold values from -0.09375 to 0.09375
- initial_state: float32 [4096], P('hid'), may hold values from -0.9 to 0.9
- guess: bfloat16 [8192, 4096], P('tm', 'hid'), may hold values from -0.8984375 to 0.8984375
Outputs:
- trajectory: bfloat16 [8192, 4096], P('tm', 'hid')
All inputs are finite; a program needn't handle non-finite values.
Results may differ from a plain program's by a relative error of at most 0.003.
Values may be sent and summed in bfloat16 or wider, within the bound.
A program may use at most 128 MiB of HBM per device.

v0:
```python
import jax
import jax.numpy as jnp
from jax import lax
from jax.sharding import PartitionSpec as P

ITERS = 2


def from_behind(x, axis, by):
    size = lax.axis_size(axis)
    pairs = [(i, i + by) for i in range(size) if 0 <= i + by < size]
    return lax.ppermute(x, axis, pairs)


def prefix(value, axis, join, neutral):
    count, mine = (lax.axis_size(axis), lax.axis_index(axis))
    pieces = jax.tree.map(lambda part: lax.all_gather(part, axis), value)
    total = jax.tree.map(
        lambda part, zero: jnp.full_like(part, 0) + jnp.asarray(zero, part.dtype), value, neutral
    )

    def turn(position, total):
        longer = join(total, jax.tree.map(lambda part: part[position], pieces))
        return jax.tree.map(lambda new, old: jnp.where(position < mine, new, old), longer, total)

    return lax.fori_loop(0, count - 1, turn, total)


def compose(earlier, later):
    earlier_gain, earlier_shift = earlier
    later_gain, later_shift = later
    return (later_gain * earlier_gain, later_gain * earlier_shift + later_shift)


def boundary_row(states):
    return from_behind(states[-1], "tm", 1)


def per_device(gate_inputs, recurrent, initial_state, guess):
    rows = gate_inputs.shape[0]
    own = recurrent.shape[2]
    hid_index = lax.axis_index("hid")
    time_index = lax.axis_index("tm")
    own_block = lax.dynamic_slice_in_dim(recurrent, hid_index * own, own, 1)
    diagonal = jnp.diagonal(own_block, axis1=1, axis2=2).astype(jnp.float32)
    inputs = gate_inputs.astype(jnp.float32)
    states = guess.astype(jnp.float32)
    entering = initial_state
    for step in range(ITERS):
        incoming = jnp.where(time_index == 0, initial_state, boundary_row(states))
        previous = jnp.concatenate([incoming[None, :], states[:-1]], axis=0)
        empty = jnp.zeros((rows, 3, own), jnp.float32)
        piece = lax.all_gather(previous.astype(jnp.bfloat16), "hid", axis=1, tiled=True)
        weight_rows = lax.slice_in_dim(recurrent, 0, piece.shape[1], axis=1)
        total = empty + jnp.einsum(
            "tk,gko->tgo", piece, weight_rows, preferred_element_type=jnp.float32
        )
        memory = total[:, 2]
        update = jax.nn.sigmoid(inputs[:, 0] + total[:, 0])
        reset = jax.nn.sigmoid(inputs[:, 1] + total[:, 1])
        candidate = jnp.tanh(inputs[:, 2] + reset * memory)
        target = (1.0 - update) * candidate + update * previous
        slope = (
            update * (1.0 - update) * diagonal[0] * (previous - candidate)
            + (1.0 - update)
            * (1.0 - candidate * candidate)
            * (reset * (1.0 - reset) * diagonal[1] * memory + reset * diagonal[2])
            + update
        )
        offset = target - slope * previous
        gains, shifts = lax.associative_scan(compose, (slope, offset), axis=0)
        identity = (jnp.ones((own,), jnp.float32), jnp.zeros((own,), jnp.float32))
        before_gain, before_shift = prefix((gains[-1], shifts[-1]), "tm", compose, identity)
        entering = before_gain * initial_state + before_shift
        states = gains * entering[None, :] + shifts
    return states.astype(jnp.bfloat16)


def solution(mesh):
    in_specs = (P("tm", None, "hid"), P(None, None, "hid"), P("hid"), P("tm", "hid"))
    out_specs = P("tm", "hid")
    return jax.shard_map(
        per_device, mesh=mesh, in_specs=in_specs, out_specs=out_specs, check_vma=False
    )
```

profile of v0, /device:TPU:1, one launch (start us, length us, event | category | flops | bytes accessed | tf_op | source)
XLA Modules:
  0.0 480.0 jit_solution(14330377499558345989)
XLA Ops:
  7.3 4.5 collective-permute-start
  14.1 6.1 %constant_dynamic-slice_fusion.4 = bf16[3,1024,1024]{2,1,0:T(8,128)(2,1)} fusion(bf16[3,4096,1024]{2,1,0:T(8,128)(2,1)} %param.9, s32[]{:T(128)S(6)} %select_n.77), kind=kLoop, calls=%fused_computation.194 | loop fusion | bytes 12582916 | tf_op jit(solution)/shard_map/dynamic_slice | solution.py:44
  20.3 11.5 %copy.12 = bf16[3,1024,1024]{2,0,1:T(4,128)(2,1)} copy(bf16[3,1024,1024]{2,1,0:T(8,128)(2,1)} %constant_dynamic-slice_fusion.4) | data formatting | bytes 12582912
  33.6 12.5 %gather_fusion = bf16[1024,3]{0,1:T(4,128)(2,1)S(1)} fusion(bf16[3,1024,1024]{2,0,1:T(4,128)(2,1)} %copy.12, s32[1024]{0:T(1024)S(1)} %bitcast.117), kind=kCustom, calls=%fused_computation | custom fusion | bytes 20480 | tf_op jit(solution)/shard_map/jit(diagonal)/gather | solution.py:45
  47.6 12.3 %fusion.2 = f32[256,3,1024]{2,0,1:T(8,128)S(1)} fusion(bf16[3,4096,1024]{2,1,0:T(8,128)(2,1)} %param.9, bf16[256,4096]{1,0:T(8,128)(2,1)} %all-gather.7.cloned.1.call-done), kind=kOutput, calls=%fused_computation.11 | convolution fusion | flops 6442450944 | bytes 30408704 | tf_op jit(solution)/shard_map/tk,gko->tgo/dot_general | solution.py:55
  59.9 2.6 fusion.10
  62.4 3.3 slice.539
  65.7 3.2 slice.540
  68.9 3.2 slice.576
  72.2 3.2 slice.577
  75.4 2.7 fusion.69
  84.9 2.0 fusion.71
  147.0 3.3 slice.538
  150.3 3.3 slice.611
  162.9 2.2 pad.205
  169.8 2.4 pad.223
  172.1 2.3 pad.207
  180.3 2.1 add_multiply_fusion.7
  183.1 2.6 pad.224
  185.7 2.6 pad.225
  188.3 2.1 add.501
  190.3 4.6 pad.227
  196.6 2.6 pad.208
  200.9 2.1 add.478
  203.0 2.9 add_multiply_fusion.3
  206.8 4.6 pad.226
  212.2 25.9 %all-gather.1 = f32[32,1,1024]{2,1,0:T(1,128)S(1)} all-gather(f32[1,1,1024]{2,1,0:T(1,128)S(1)} %add_bitcast_fusion.2), channel_id=1, replica_groups=mesh['tm'=32,'hid'=4] {'tm'}, dimensions={0}, use_global_device_ids=true | all-gather | bytes 135168 | tf_op jit(solution)/shard_map/all_gather | solution.py:17
  238.1 4.6 pad.211
  242.7 1.9 pad_maximum_fusion.2
  244.6 4.7 pad.210
  250.1 23.1 %all-gather = f32[32,1,1024]{2,1,0:T(1,128)S(1)} all-gather(f32[1,1,1024]{2,1,0:T(1,128)S(1)} %add_bitcast_fusion.3), channel_id=1, replica_groups=mesh['tm'=32,'hid'=4] {'tm'}, dimensions={0}, use_global_device_ids=true | all-gather | bytes 135168 | tf_op jit(solution)/shard_map/all_gather | solution.py:17
  273.2 1.8 while.32
  275.1 2.6 multiply_add_fusion
  277.8 2.3 collective-permute-start.1
  281.8 33.1 %all-gather.9.cloned.1.call-done = bf16[256,4096]{1,0:T(8,128)(2,1)} async-done(((bf16[256,1024]{1,0:T(8,128)(2,1)}), bf16[256,4096]{1,0:T(8,128)(2,1)}) %all-gather.9.cloned.1.call-update) | async-done | bytes 2097168 | tf_op jit(solution)/shard_map/all_gather | solution.py:53
  314.9 12.3 %fusion = f32[256,3,1024]{2,0,1:T(8,128)S(1)} fusion(bf16[3,4096,1024]{2,1,0:T(8,128)(2,1)} %param.9, bf16[256,4096]{1,0:T(8,128)(2,1)} %all-gather.9.cloned.1.call-done), kind=kOutput, calls=%fused_computation.9 | convolution fusion | flops 6442450944 | bytes 30408704 | tf_op jit(solution)/shard_map/tk,gko->tgo/dot_general | solution.py:55
  327.2 2.6 fusion.17
  329.8 2.2 slice.620
  332.0 2.1 slice.621
  334.0 3.2 slice.657
  407.9 2.3 add_multiply_fusion.1
  410.4 25.1 %all-gather.3 = f32[32,1,1024]{2,1,0:T(1,128)S(1)} all-gather(f32[1,1,1024]{2,1,0:T(1,128)S(1)} %add_bitcast_fusion), channel_id=1, replica_groups=mesh['tm'=32,'hid'=4] {'tm'}, dimensions={0}, use_global_device_ids=true | all-gather | bytes 135168 | tf_op jit(solution)/shard_map/all_gather | solution.py:17
  435.5 2.1 pad.243
  437.6 1.9 pad_maximum_fusion.4
  439.5 4.6 pad.242
  444.9 23.9 %all-gather.2 = f32[32,1,1024]{2,1,0:T(1,128)S(1)} all-gather(f32[1,1,1024]{2,1,0:T(1,128)S(1)} %add_bitcast_fusion.1), channel_id=1, replica_groups=mesh['tm'=32,'hid'=4] {'tm'}, dimensions={0}, use_global_device_ids=true | all-gather | bytes 135168 | tf_op jit(solution)/shard_map/all_gather | solution.py:17
  468.8 1.8 while.33
  470.7 2.5 add_convert_fusion
  (468 shorter events, 173.2 us)
Async XLA Ops:
  6.5 41.0 %all-gather.7.cloned.1.call-start = ((), (), s32[]{:S(2)}) async-start(), calls=%async_computation | async-start | bytes 2621440 | tf_op jit(solution)/shard_map/all_gather | solution.py:53
  7.3 5.7 %collective-permute-start = (f32[1024]{0:T(1024)S(1)}, f32[1024]{0:T(1024)S(1)}, u32[]{:S(2)}, u32[]{:S(2)}) collective-permute-start(f32[1024]{0:T(1024)S(1)} %bitcast.138), channel_id=1, source_target_pairs={{0,4},{4,8},{8,12},{12,16},{16,20},{20,24},{24,28},{28,32},{32,36}... | collective-permute-start | bytes 12296 | tf_op jit(solution)/shard_map/ppermute | solution.py:12
  12.9 7.3 %copy-start.2 = (f32[255,1024]{1,0:T(8,128)}, f32[255,1024]{1,0:T(8,128)S(1)}, u32[]{:S(2)}) copy-start(f32[255,1024]{1,0:T(8,128)S(1)} %slice.698) | copy-start | bytes 3133444
  14.1 300.8 %all-gather.9.cloned.1.call-start = ((), (), s32[]{:S(2)}) async-start(), calls=%async_computation.1 | async-start | bytes 2621440 | tf_op jit(solution)/shard_map/all_gather | solution.py:53
  46.2 13.6 %copy-start.20 = (f32[1,1024]{1,0:T(1,128)}, f32[1,1024]{1,0:T(1,128)S(1)}, u32[]{:S(2)}) copy-start(f32[1,1024]{1,0:T(1,128)S(1)} %get-tuple-element.364) | copy-start | bytes 12292
  46.2 13.6 %copy-start.22 = (f32[1,1024]{1,0:T(1,128)}, f32[1,1024]{1,0:T(1,128)S(1)}, u32[]{:S(2)}) copy-start(f32[1,1024]{1,0:T(1,128)S(1)} %get-tuple-element.365) | copy-start | bytes 12292
  47.6 12.3 %copy-start.3 = (f32[255,1024]{1,0:T(8,128)S(1)}, f32[255,1024]{1,0:T(8,128)}, u32[]{:S(2)}) copy-start(f32[255,1024]{1,0:T(8,128)} %copy-done.2) | copy-start | bytes 3133444
  136.5 19.7 %copy-start.13 = (f32[7,1024]{1,0:T(8,128)S(1)}, f32[7,1024]{1,0:T(8,128)}, u32[]{:S(2)}) copy-start(f32[7,1024]{1,0:T(8,128)} %slice.554) | copy-start | bytes 86020
  136.5 19.7 %copy-start.14 = (f32[7,1024]{1,0:T(8,128)S(1)}, f32[7,1024]{1,0:T(8,128)}, u32[]{:S(2)}) copy-start(f32[7,1024]{1,0:T(8,128)} %slice.603) | copy-start | bytes 86020
  136.5 21.8 %copy-start.10 = (f32[15,1024]{1,0:T(8,128)S(1)}, f32[15,1024]{1,0:T(8,128)}, u32[]{:S(2)}) copy-start(f32[15,1024]{1,0:T(8,128)} %slice.550) | copy-start | bytes 184324
  140.8 14.9 %copy-start.27 = (f32[2,1024]{1,0:T(2,128)S(1)}, f32[2,1024]{1,0:T(2,128)}, u32[]{:S(2)}) copy-start(f32[2,1024]{1,0:T(2,128)} %get-tuple-element.379) | copy-start | bytes 24580
  140.8 14.9 %copy-start.26 = (f32[2,1024]{1,0:T(2,128)S(1)}, f32[2,1024]{1,0:T(2,128)}, u32[]{:S(2)}) copy-start(f32[2,1024]{1,0:T(2,128)} %get-tuple-element.378) | copy-start | bytes 24580
  140.8 15.0 %copy-start.45 = (f32[1,1024]{1,0:T(1,128)S(1)}, f32[1,1024]{1,0:T(1,128)}, u32[]{:S(2)}) copy-start(f32[1,1024]{1,0:T(1,128)} %get-tuple-element.357) | copy-start | bytes 12292
  140.8 15.0 %copy-start.46 = (f32[1,1024]{1,0:T(1,128)S(1)}, f32[1,1024]{1,0:T(1,128)}, u32[]{:S(2)}) copy-start(f32[1,1024]{1,0:T(1,128)} %get-tuple-element.358) | copy-start | bytes 12292
  140.8 15.0 %copy-start.47 = (f32[1,1024]{1,0:T(1,128)S(1)}, f32[1,1024]{1,0:T(1,128)}, u32[]{:S(2)}) copy-start(f32[1,1024]{1,0:T(1,128)} %get-tuple-element.359) | copy-start | bytes 12292
  140.8 15.0 %copy-start.48 = (f32[1,1024]{1,0:T(1,128)S(1)}, f32[1,1024]{1,0:T(1,128)}, u32[]{:S(2)}) copy-start(f32[1,1024]{1,0:T(1,128)} %get-tuple-element.360) | copy-start | bytes 12292
  140.8 15.1 %copy-start.18 = (f32[3,1024]{1,0:T(4,128)S(1)}, f32[3,1024]{1,0:T(4,128)}, u32[]{:S(2)}) copy-start(f32[3,1024]{1,0:T(4,128)} %slice.558) | copy-start | bytes 36868
  140.8 15.1 %copy-start.19 = (f32[3,1024]{1,0:T(4,128)S(1)}, f32[3,1024]{1,0:T(4,128)}, u32[]{:S(2)}) copy-start(f32[3,1024]{1,0:T(4,128)} %slice.601) | copy-start | bytes 36868
  140.8 15.1 %copy-start.40 = (f32[1,1024]{1,0:T(1,128)S(1)}, f32[1,1024]{1,0:T(1,128)}, u32[]{:S(2)}) copy-start(f32[1,1024]{1,0:T(1,128)} %slice.738) | copy-start | bytes 12292
  140.9 15.2 %copy-start.39 = (f32[1,1024]{1,0:T(1,128)S(1)}, f32[1,1024]{1,0:T(1,128)}, u32[]{:S(2)}) copy-start(f32[1,1024]{1,0:T(1,128)} %slice.712) | copy-start | bytes 12292
  176.8 5.5 %copy-start.32 = (f32[1,1024]{1,0:T(1,128)S(1)}, f32[1,1024]{1,0:T(1,128)}, u32[]{:S(2)}) copy-start(f32[1,1024]{1,0:T(1,128)} %slice.734) | copy-start | bytes 12292
  182.3 12.6 %copy-start.30 = (f32[1,1024]{1,0:T(1,128)S(1)}, f32[1,1024]{1,0:T(1,128)}, u32[]{:S(2)}) copy-start(f32[1,1024]{1,0:T(1,128)} %slice.708) | copy-start | bytes 12292
  183.1 16.2 %copy-start.6 = (f32[64,1024]{1,0:T(8,128)S(1)}, f32[64,1024]{1,0:T(8,128)}, u32[]{:S(2)}) copy-start(f32[64,1024]{1,0:T(8,128)} %add.477) | copy-start | bytes 786436
  205.9 36.8 %copy-start.28 = (f32[1,1024]{1,0:T(1,128)S(1)}, f32[1,1024]{1,0:T(1,128)}, u32[]{:S(2)}) copy-start(f32[1,1024]{1,0:T(1,128)} %slice.707) | copy-start | bytes 12292
  206.8 68.3 %copy-start.17 = (f32[1024]{0:T(1024)S(1)}, f32[1024]{0:T(1024)}, u32[]{:S(2)}) copy-start(f32[1024]{0:T(1024)} %param.10) | copy-start | bytes 12292
  277.7 3.1 copy-start
  277.8 3.1 collective-permute-start.1
  281.8 45.4 %copy-start.21 = (f32[1,1024]{1,0:T(1,128)S(1)}, f32[1,1024]{1,0:T(1,128)}, u32[]{:S(2)}) copy-start(f32[1,1024]{1,0:T(1,128)} %copy-done.20) | copy-start | bytes 12292
  281.8 45.4 %copy-start.23 = (f32[1,1024]{1,0:T(1,128)S(1)}, f32[1,1024]{1,0:T(1,128)}, u32[]{:S(2)}) copy-start(f32[1,1024]{1,0:T(1,128)} %copy-done.22) | copy-start | bytes 12292
  314.9 12.3 %copy-start.1 = (f32[256,1024]{1,0:T(8,128)S(1)}, f32[256,1024]{1,0:T(8,128)}, u32[]{:S(2)}) copy-start(f32[256,1024]{1,0:T(8,128)} %copy-done) | copy-start | bytes 3145732
  329.8 7.5 %copy-start.5 = (f32[256,1024]{1,0:T(8,128)S(1)}, f32[256,1024]{1,0:T(8,128)}, u32[]{:S(2)}) copy-start(f32[256,1024]{1,0:T(8,128)} %get-tuple-element.295) | copy-start | bytes 3145732
  341.5 56.8 %copy-start.4 = (f32[256,1024]{1,0:T(8,128)S(1)}, f32[256,1024]{1,0:T(8,128)}, u32[]{:S(2)}) copy-start(f32[256,1024]{1,0:T(8,128)} %get-tuple-element.296) | copy-start | bytes 3145732
  395.4 6.6 %copy-start.43 = (f32[1,1024]{1,0:T(1,128)S(1)}, f32[1,1024]{1,0:T(1,128)}, u32[]{:S(2)}) copy-start(f32[1,1024]{1,0:T(1,128)} %get-tuple-element.350) | copy-start | bytes 12292
  395.4 6.6 %copy-start.44 = (f32[1,1024]{1,0:T(1,128)S(1)}, f32[1,1024]{1,0:T(1,128)}, u32[]{:S(2)}) copy-start(f32[1,1024]{1,0:T(1,128)} %get-tuple-element.351) | copy-start | bytes 12292
  395.4 6.6 %copy-start.24 = (f32[2,1024]{1,0:T(2,128)S(1)}, f32[2,1024]{1,0:T(2,128)}, u32[]{:S(2)}) copy-start(f32[2,1024]{1,0:T(2,128)} %pad_add_fusion) | copy-start | bytes 24580
  395.4 6.6 %copy-start.25 = (f32[2,1024]{1,0:T(2,128)S(1)}, f32[2,1024]{1,0:T(2,128)}, u32[]{:S(2)}) copy-start(f32[2,1024]{1,0:T(2,128)} %pad_add_fusion.1) | copy-start | bytes 24580
  395.4 6.7 %copy-start.41 = (f32[1,1024]{1,0:T(1,128)S(1)}, f32[1,1024]{1,0:T(1,128)}, u32[]{:S(2)}) copy-start(f32[1,1024]{1,0:T(1,128)} %get-tuple-element.349) | copy-start | bytes 12292
  395.4 6.7 %copy-start.42 = (f32[1,1024]{1,0:T(1,128)S(1)}, f32[1,1024]{1,0:T(1,128)}, u32[]{:S(2)}) copy-start(f32[1,1024]{1,0:T(1,128)} %get-tuple-element.352) | copy-start | bytes 12292
  395.4 9.0 %copy-start.15 = (f32[7,1024]{1,0:T(8,128)S(1)}, f32[7,1024]{1,0:T(8,128)}, u32[]{:S(2)}) copy-start(f32[7,1024]{1,0:T(8,128)} %slice.635) | copy-start | bytes 86020
  395.4 9.0 %copy-start.16 = (f32[7,1024]{1,0:T(8,128)S(1)}, f32[7,1024]{1,0:T(8,128)}, u32[]{:S(2)}) copy-start(f32[7,1024]{1,0:T(8,128)} %slice.684) | copy-start | bytes 86020
  395.4 9.2 %copy-start.11 = (f32[15,1024]{1,0:T(8,128)S(1)}, f32[15,1024]{1,0:T(8,128)}, u32[]{:S(2)}) copy-start(f32[15,1024]{1,0:T(8,128)} %slice.631) | copy-start | bytes 184324
  395.4 9.2 %copy-start.12 = (f32[15,1024]{1,0:T(8,128)S(1)}, f32[15,1024]{1,0:T(8,128)}, u32[]{:S(2)}) copy-start(f32[15,1024]{1,0:T(8,128)} %slice.686) | copy-start | bytes 184324
  397.7 6.8 %copy-start.38 = (f32[1,1024]{1,0:T(1,128)S(1)}, f32[1,1024]{1,0:T(1,128)}, u32[]{:S(2)}) copy-start(f32[1,1024]{1,0:T(1,128)} %slice.794) | copy-start | bytes 12292
  397.7 6.9 %copy-start.37 = (f32[1,1024]{1,0:T(1,128)S(1)}, f32[1,1024]{1,0:T(1,128)}, u32[]{:S(2)}) copy-start(f32[1,1024]{1,0:T(1,128)} %slice.768) | copy-start | bytes 12292
  397.7 7.0 %copy-start.36 = (f32[1,1024]{1,0:T(1,128)S(1)}, f32[1,1024]{1,0:T(1,128)}, u32[]{:S(2)}) copy-start(f32[1,1024]{1,0:T(1,128)} %slice.793) | copy-start | bytes 12292
  398.3 7.4 %copy-start.9 = (f32[31,1024]{1,0:T(8,128)S(1)}, f32[31,1024]{1,0:T(8,128)}, u32[]{:S(2)}) copy-start(f32[31,1024]{1,0:T(8,128)} %slice.688) | copy-start | bytes 380932
  399.8 5.9 %copy-start.35 = (f32[1,1024]{1,0:T(1,128)S(1)}, f32[1,1024]{1,0:T(1,128)}, u32[]{:S(2)}) copy-start(f32[1,1024]{1,0:T(1,128)} %slice.792) | copy-start | bytes 12292
  407.0 3.2 copy-start.29
  (5 other events, 5.5 us)
Sparse Core Ops, SparseCore 0:
  14.2 33.3 all-gather.6
  281.9 32.9 all-gather.8
where the time goes:
time: 487 us; the launch traced here: 480 us
  local copies, waits for them, and re-layouts  218 us (45%)
  blocking collectives  98 us (20%)
  other arithmetic  79.8 us (16%)
  waiting for transfers between devices  35.2 us (7%)
  matrix products  24.5 us (5%)
  between operations  14.8 us (3%)
  starting transfers between devices  6.89 us (1%)
    slice x104, local copies, waits for them, and re-layouts, per_device(): gains, shifts = lax.associative_scan(compose, (slope, offset), axis=0)  140 us
    all_gather x4, blocking collectives, prefix(): pieces = jax.tree.map(lambda part: lax.all_gather(part, axis), value)  98 us
    pad x56, local copies, waits for them, and re-layouts, per_device(): gains, shifts = lax.associative_scan(compose, (slope, offset), axis=0)  45.2 us
    all_gather x2, waiting for transfers between devices, per_device(): lax.all_gather(previous.astype(jnp.bfloat16), 'hid', axis=1, tiled=True)  34.4 us
    mul x26, other arithmetic, compose(): return (later_gain * earlier_gain, later_gain * earlier_shift + later_shift)  32.1 us
    dot_general x2, matrix products, per_device(): jnp.einsum('tk,gko->tgo', piece, weight_rows, preferred_element_type=jnp....  24.5 us
    concatenate x27, other arithmetic, per_device(): gains, shifts = lax.associative_scan(compose, (slope, offset), axis=0)  14.6 us
    add x27, other arithmetic, per_device(): gains, shifts = lax.associative_scan(compose, (slope, offset), axis=0)  13.4 us
  transfers between devices with their start and end apart: 4, of which 3 were waited for; matrix products, arithmetic and copies ran while one was open for 7% of the time, Pallas kernels for 0%

commit v1 on v0

--- a/solution.py
+++ b/solution.py
@@ -50,7 +50,24 @@
         incoming = jnp.where(time_index == 0, initial_state, boundary_row(states))
         previous = jnp.concatenate([incoming[None, :], states[:-1]], axis=0)
         empty = jnp.zeros((rows, 3, own), jnp.float32)
-        piece = lax.all_gather(previous.astype(jnp.bfloat16), "hid", axis=1, tiled=True)
+        array = previous.astype(jnp.bfloat16)
+        devices, mine_2, extent = (lax.axis_size("hid"), lax.axis_index("hid"), array.shape[1])
+        upward = [(i_2, (i_2 + 1) % devices) for i_2 in range(devices)]
+        behind = [(i_2, (i_2 - 1) % devices) for i_2 in range(devices)]
+        piece = jnp.zeros((*array.shape[:1], devices * extent, *array.shape[1 + 1 :]), array.dtype)
+        piece = lax.dynamic_update_slice_in_dim(piece, array, mine_2 * extent, axis=1)
+        from_left = from_right = array
+        half = devices // 2
+        for k in range(1, half + 1):
+            from_left = lax.ppermute(from_left, "hid", upward)
+            piece = lax.dynamic_update_slice_in_dim(
+                piece, from_left, (mine_2 - k) % devices * extent, axis=1
+            )
+            if k < devices - half:
+                from_right = lax.ppermute(from_right, "hid", behind)
+                piece = lax.dynamic_update_slice_in_dim(
+                    piece, from_right, (mine_2 + k) % devices * extent, axis=1
+                )
         weight_rows = lax.slice_in_dim(recurrent, 0, piece.shape[1], axis=1)
         total = empty + jnp.einsum(
             "tk,gko->tgo", piece, weight_rows, preferred_element_type=jnp.float32

time: 487 us -> 486 us (level)
  between operations: 14.8 us -> 1.4 us
  local copies, waits for them, and re-layouts: 218 us -> 228 us
  starting transfers between devices: 6.89 us -> 13.3 us
    all_gather x2 -> x0, waiting for transfers between devices: 34.4 us -> none  [per_device(): lax.all_gather(previous.astype(jnp.bfloat16), 'hid', axis=1, tiled=True)]
    ppermute x0 -> x6, waiting for transfers between devices: none -> 31.2 us  [the longest x4 23.5 us: per_device(): from_left = lax.ppermute(from_left, 'hid', upward)]
    dynamic_update_slice x0 -> x6, local copies, waits for them, and re-layouts: none -> 11.5 us  [the longest x4 7.64 us: per_device(): lax.dynamic_update_slice_in_dim(piece, from_left, (mine_2 - k) % devices...]
    ppermute x0 -> x6, starting transfers between devices: none -> 6.52 us  [the longest x2 4.65 us: per_device(): from_right = lax.ppermute(from_right, 'hid', behind)]
  transfers between devices with their start and end apart: 4 -> 8, of which waited for: 3 -> 5; matrix products, arithmetic and copies ran while one was open for 7% -> 8% of each run, Pallas kernels for 0% -> 0%
where the time goes in v1:
time: 486 us; the launch traced here: 479 us
  local copies, waits for them, and re-layouts  228 us (47%)
  blocking collectives  96.7 us (20%)
  other arithmetic  80.1 us (16%)
  waiting for transfers between devices  32 us (7%)
  matrix products  24.5 us (5%)
  starting transfers between devices  13.3 us (3%)
    slice x104, local copies, waits for them, and re-layouts, per_device(): gains, shifts = lax.associative_scan(compose, (slope, offset), axis=0)  135 us
    all_gather x4, blocking collectives, prefix(): pieces = jax.tree.map(lambda part: lax.all_gather(part, axis), value)  96.7 us
    pad x56, local copies, waits for them, and re-layouts, per_device(): gains, shifts = lax.associative_scan(compose, (slope, offset), axis=0)  44.4 us
    mul x26, other arithmetic, compose(): return (later_gain * earlier_gain, later_gain * earlier_shift + later_shift)  30.5 us
    dot_general x2, matrix products, per_device(): jnp.einsum('tk,gko->tgo', piece, weight_rows, preferred_element_type=jnp....  24.5 us
    ppermute x4, waiting for transfers between devices, per_device(): from_left = lax.ppermute(from_left, 'hid', upward)  23.5 us
    concatenate x27, other arithmetic, per_device(): gains, shifts = lax.associative_scan(compose, (slope, offset), axis=0)  16.6 us
    unnamed x103, local copies, waits for them, and re-layouts  16 us
  transfers between devices with their start and end apart: 8, of which 5 were waited for; matrix products, arithmetic and copies ran while one was open for 8% of the time, Pallas kernels for 0%

profile of v1, /device:TPU:1, one launch (start us, length us, event | category | flops | bytes accessed | tf_op | source)
XLA Modules:
  0.0 478.7 jit_solution(2321718321772560847)
XLA Ops:
  0.7 4.5 collective-permute-start
  10.6 6.1 %constant_dynamic-slice_fusion.4 = bf16[3,1024,1024]{2,1,0:T(8,128)(2,1)} fusion(bf16[3,4096,1024]{2,1,0:T(8,128)(2,1)} %param.9, s32[]{:T(128)S(6)} %select_n.112), kind=kLoop, calls=%fused_computation.194 | loop fusion | bytes 12582916 | tf_op jit(solution)/shard_map/dynamic_slice | solution.py:44
  16.7 11.5 %copy.12 = bf16[3,1024,1024]{2,0,1:T(4,128)(2,1)} copy(bf16[3,1024,1024]{2,1,0:T(8,128)(2,1)} %constant_dynamic-slice_fusion.4) | data formatting | bytes 12582912
  28.3 12.3 %gather_fusion = bf16[1024,3]{0,1:T(4,128)(2,1)S(1)} fusion(bf16[3,1024,1024]{2,0,1:T(4,128)(2,1)} %copy.12, s32[1024]{0:T(1024)S(1)} %bitcast.117), kind=kCustom, calls=%fused_computation | custom fusion | bytes 20480 | tf_op jit(solution)/shard_map/jit(diagonal)/gather | solution.py:45
  40.6 2.2 collective-permute-start.2
  46.6 7.7 %collective-permute-done.2 = bf16[256,1024]{1,0:T(8,128)(2,1)} collective-permute-done((bf16[256,1024]{1,0:T(8,128)(2,1)}, bf16[256,1024]{1,0:T(8,128)(2,1)}, u32[]{:S(2)}, u32[]{:S(2)}) %collective-permute-start.2) | collective-permute-done | bytes 524320 | tf_op jit(solution)/shard_map/ppermute | solution.py:67
  59.3 12.3 %fusion.2 = f32[256,3,1024]{2,0,1:T(8,128)S(1)} fusion(bf16[3,4096,1024]{2,1,0:T(8,128)(2,1)} %param.9, bf16[256,4096]{1,0:T(8,128)(2,1)} %constant_dynamic-update-slice_fusion.4), kind=kOutput, calls=%fused_computation.11 | convolution fusion | flops 6442450944 | bytes 30408704 | tf_op jit(solution)/shard_map/tk,gko->tgo/dot_general | solution.py:72
  71.6 2.6 fusion.10
  74.2 3.3 slice.539
  77.5 3.3 slice.540
  80.8 3.3 slice.576
  84.0 3.3 slice.577
  87.3 2.7 fusion.71
  96.8 2.0 fusion.73
  158.9 3.3 slice.538
  162.2 3.3 slice.611
  176.0 2.2 pad.205
  182.9 2.4 pad.223
  185.3 2.4 pad.207
  193.5 2.0 add_multiply_fusion.7
  197.2 2.6 pad.225
  199.8 2.1 add.541
  202.0 4.6 pad.227
  208.2 2.6 pad.208
  212.6 2.1 add.518
  214.7 2.9 add_multiply_fusion.3
  218.4 4.6 pad.226
  223.8 25.7 %all-gather.1 = f32[32,1,1024]{2,1,0:T(1,128)S(1)} all-gather(f32[1,1,1024]{2,1,0:T(1,128)S(1)} %add_bitcast_fusion.2), channel_id=1, replica_groups=mesh['tm'=32,'hid'=4] {'tm'}, dimensions={0}, use_global_device_ids=true | all-gather | bytes 135168 | tf_op jit(solution)/shard_map/all_gather | solution.py:17
  249.5 4.6 pad.211
  256.0 4.7 pad.210
  261.5 23.0 %all-gather = f32[32,1,1024]{2,1,0:T(1,128)S(1)} all-gather(f32[1,1,1024]{2,1,0:T(1,128)S(1)} %add_bitcast_fusion.3), channel_id=1, replica_groups=mesh['tm'=32,'hid'=4] {'tm'}, dimensions={0}, use_global_device_ids=true | all-gather | bytes 135168 | tf_op jit(solution)/shard_map/all_gather | solution.py:17
  286.4 2.6 multiply_add_fusion
  289.0 2.3 collective-permute-start.4
  294.8 2.5 collective-permute-start.6
  297.2 12.2 %collective-permute-done.5 = bf16[256,1024]{1,0:T(8,128)(2,1)} collective-permute-done((bf16[256,1024]{1,0:T(8,128)(2,1)}, bf16[256,1024]{1,0:T(8,128)(2,1)}, u32[]{:S(2)}, u32[]{:S(2)}) %collective-permute-start.5) | collective-permute-done | bytes 524320 | tf_op jit(solution)/shard_map/ppermute | solution.py:62
  309.5 1.9 constant_dynamic-update-slice_fusion.2
  311.4 2.0 constant_dynamic-update-slice_fusion.1
  313.3 10.1 %collective-permute-done.7 = bf16[256,1024]{1,0:T(8,128)(2,1)} collective-permute-done((bf16[256,1024]{1,0:T(8,128)(2,1)}, bf16[256,1024]{1,0:T(8,128)(2,1)}, u32[]{:S(2)}, u32[]{:S(2)}) %collective-permute-start.7) | collective-permute-done | bytes 524320 | tf_op jit(solution)/shard_map/ppermute | solution.py:62
  325.3 12.3 %fusion = f32[256,3,1024]{2,0,1:T(8,128)S(1)} fusion(bf16[3,4096,1024]{2,1,0:T(8,128)(2,1)} %param.9, bf16[256,4096]{1,0:T(8,128)(2,1)} %constant_dynamic-update-slice_fusion), kind=kOutput, calls=%fused_computation.9 | convolution fusion | flops 6442450944 | bytes 30408704 | tf_op jit(solution)/shard_map/tk,gko->tgo/dot_general | solution.py:72
  337.6 2.6 fusion.17
  340.2 2.2 slice.620
  342.4 2.1 slice.621
  414.4 2.3 add_multiply_fusion.1
  416.9 26.1 %all-gather.3 = f32[32,1,1024]{2,1,0:T(1,128)S(1)} all-gather(f32[1,1,1024]{2,1,0:T(1,128)S(1)} %add_bitcast_fusion), channel_id=1, replica_groups=mesh['tm'=32,'hid'=4] {'tm'}, dimensions={0}, use_global_device_ids=true | all-gather | bytes 135168 | tf_op jit(solution)/shard_map/all_gather | solution.py:17
  443.0 2.1 pad.243
  447.0 4.6 pad.242
  452.4 22.0 %all-gather.2 = f32[32,1,1024]{2,1,0:T(1,128)S(1)} all-gather(f32[1,1,1024]{2,1,0:T(1,128)S(1)} %add_bitcast_fusion.1), channel_id=1, replica_groups=mesh['tm'=32,'hid'=4] {'tm'}, dimensions={0}, use_global_device_ids=true | all-gather | bytes 135168 | tf_op jit(solution)/shard_map/all_gather | solution.py:17
  476.3 2.5 add_convert_fusion
  (482 shorter events, 194.6 us)
Async XLA Ops:
  0.0 6.4 %copy-start.20 = (f32[1024]{0:T(1024)S(1)}, f32[1024]{0:T(1024)}, u32[]{:S(2)}) copy-start(f32[1024]{0:T(1024)} %param.10) | copy-start | bytes 12292
  0.7 5.7 %collective-permute-start = (f32[1024]{0:T(1024)S(1)}, f32[1024]{0:T(1024)S(1)}, u32[]{:S(2)}, u32[]{:S(2)}) collective-permute-start(f32[1024]{0:T(1024)S(1)} %bitcast.138), channel_id=1, source_target_pairs={{0,4},{4,8},{8,12},{12,16},{16,20},{20,24},{24,28},{28,32},{32,36}... | collective-permute-start | bytes 12296 | tf_op jit(solution)/shard_map/ppermute | solution.py:12
  7.6 1.3 copy-start.7
  9.0 33.8 %collective-permute-start.1 = (bf16[256,1024]{1,0:T(8,128)(2,1)}, bf16[256,1024]{1,0:T(8,128)(2,1)}, u32[]{:S(2)}, u32[]{:S(2)}) collective-permute-start(bf16[256,1024]{1,0:T(8,128)(2,1)} %get-tuple-element.302), channel_id=1, source_target_pairs={{0,1},{1,2},{2,3},{3,0},{4,5},{5,6},{6,7},{7,4},{8,9},{9,10},{10,1... | collective-permute-start | bytes 1572872 | tf_op jit(solution)/shard_map/ppermute | solution.py:62
  40.6 13.8 %collective-permute-start.2 = (bf16[256,1024]{1,0:T(8,128)(2,1)}, bf16[256,1024]{1,0:T(8,128)(2,1)}, u32[]{:S(2)}, u32[]{:S(2)}) collective-permute-start(bf16[256,1024]{1,0:T(8,128)(2,1)} %get-tuple-element.302), channel_id=1, source_target_pairs={{0,3},{1,0},{2,1},{3,2},{4,7},{5,4},{6,5},{7,6},{8,11},{9,8},{10,9... | collective-permute-start | bytes 1572872 | tf_op jit(solution)/shard_map/ppermute | solution.py:67
  42.8 14.7 %collective-permute-start.3 = (bf16[256,1024]{1,0:T(8,128)(2,1)}, bf16[256,1024]{1,0:T(8,128)(2,1)}, u32[]{:S(2)}, u32[]{:S(2)}) collective-permute-start(bf16[256,1024]{1,0:T(8,128)(2,1)} %collective-permute-done.1), channel_id=1, source_target_pairs={{0,1},{1,2},{2,3},{3,0},{4,5},{5,6},{6,7},{7,4},{8,9},{9,10},{10,1... | collective-permute-start | bytes 1572872 | tf_op jit(solution)/shard_map/ppermute | solution.py:62
  44.7 26.9 %copy-start.25 = (f32[1,1024]{1,0:T(1,128)}, f32[1,1024]{1,0:T(1,128)S(1)}, u32[]{:S(2)}) copy-start(f32[1,1024]{1,0:T(1,128)S(1)} %get-tuple-element.368) | copy-start | bytes 12292
  44.7 26.9 %copy-start.27 = (f32[1,1024]{1,0:T(1,128)}, f32[1,1024]{1,0:T(1,128)S(1)}, u32[]{:S(2)}) copy-start(f32[1,1024]{1,0:T(1,128)S(1)} %get-tuple-element.369) | copy-start | bytes 12292
  59.3 12.3 %copy-start.3 = (f32[255,1024]{1,0:T(8,128)S(1)}, f32[255,1024]{1,0:T(8,128)}, u32[]{:S(2)}) copy-start(f32[255,1024]{1,0:T(8,128)} %copy-done.2) | copy-start | bytes 3133444
  149.1 20.3 %copy-start.16 = (f32[7,1024]{1,0:T(8,128)S(1)}, f32[7,1024]{1,0:T(8,128)}, u32[]{:S(2)}) copy-start(f32[7,1024]{1,0:T(8,128)} %slice.554) | copy-start | bytes 86020
  149.1 20.3 %copy-start.17 = (f32[7,1024]{1,0:T(8,128)S(1)}, f32[7,1024]{1,0:T(8,128)}, u32[]{:S(2)}) copy-start(f32[7,1024]{1,0:T(8,128)} %slice.603) | copy-start | bytes 86020
  152.7 15.6 %copy-start.32 = (f32[2,1024]{1,0:T(2,128)S(1)}, f32[2,1024]{1,0:T(2,128)}, u32[]{:S(2)}) copy-start(f32[2,1024]{1,0:T(2,128)} %get-tuple-element.383) | copy-start | bytes 24580
  152.7 15.6 %copy-start.31 = (f32[2,1024]{1,0:T(2,128)S(1)}, f32[2,1024]{1,0:T(2,128)}, u32[]{:S(2)}) copy-start(f32[2,1024]{1,0:T(2,128)} %get-tuple-element.382) | copy-start | bytes 24580
  152.7 15.6 %copy-start.45 = (f32[1,1024]{1,0:T(1,128)S(1)}, f32[1,1024]{1,0:T(1,128)}, u32[]{:S(2)}) copy-start(f32[1,1024]{1,0:T(1,128)} %get-tuple-element.361) | copy-start | bytes 12292
  152.7 15.6 %copy-start.46 = (f32[1,1024]{1,0:T(1,128)S(1)}, f32[1,1024]{1,0:T(1,128)}, u32[]{:S(2)}) copy-start(f32[1,1024]{1,0:T(1,128)} %get-tuple-element.362) | copy-start | bytes 12292
  152.7 15.6 %copy-start.47 = (f32[1,1024]{1,0:T(1,128)S(1)}, f32[1,1024]{1,0:T(1,128)}, u32[]{:S(2)}) copy-start(f32[1,1024]{1,0:T(1,128)} %get-tuple-element.363) | copy-start | bytes 12292
  152.7 15.6 %copy-start.48 = (f32[1,1024]{1,0:T(1,128)S(1)}, f32[1,1024]{1,0:T(1,128)}, u32[]{:S(2)}) copy-start(f32[1,1024]{1,0:T(1,128)} %get-tuple-element.364) | copy-start | bytes 12292
  152.7 15.7 %copy-start.21 = (f32[3,1024]{1,0:T(4,128)S(1)}, f32[3,1024]{1,0:T(4,128)}, u32[]{:S(2)}) copy-start(f32[3,1024]{1,0:T(4,128)} %slice.558) | copy-start | bytes 36868
  152.7 15.7 %copy-start.22 = (f32[3,1024]{1,0:T(4,128)S(1)}, f32[3,1024]{1,0:T(4,128)}, u32[]{:S(2)}) copy-start(f32[3,1024]{1,0:T(4,128)} %slice.601) | copy-start | bytes 36868
  152.7 15.8 %copy-start.44 = (f32[1,1024]{1,0:T(1,128)S(1)}, f32[1,1024]{1,0:T(1,128)}, u32[]{:S(2)}) copy-start(f32[1,1024]{1,0:T(1,128)} %slice.738) | copy-start | bytes 12292
  156.2 15.3 %copy-start.13 = (f32[15,1024]{1,0:T(8,128)S(1)}, f32[15,1024]{1,0:T(8,128)}, u32[]{:S(2)}) copy-start(f32[15,1024]{1,0:T(8,128)} %slice.550) | copy-start | bytes 184324
  190.0 5.5 %copy-start.38 = (f32[1,1024]{1,0:T(1,128)S(1)}, f32[1,1024]{1,0:T(1,128)}, u32[]{:S(2)}) copy-start(f32[1,1024]{1,0:T(1,128)} %slice.734) | copy-start | bytes 12292
  197.2 9.4 %copy-start.36 = (f32[1,1024]{1,0:T(1,128)S(1)}, f32[1,1024]{1,0:T(1,128)}, u32[]{:S(2)}) copy-start(f32[1,1024]{1,0:T(1,128)} %slice.708) | copy-start | bytes 12292
  199.8 11.0 %copy-start.9 = (f32[64,1024]{1,0:T(8,128)S(1)}, f32[64,1024]{1,0:T(8,128)}, u32[]{:S(2)}) copy-start(f32[64,1024]{1,0:T(8,128)} %add.517) | copy-start | bytes 786436
  214.7 2.9 copy-start.34
  217.6 36.6 %copy-start.33 = (f32[1,1024]{1,0:T(1,128)S(1)}, f32[1,1024]{1,0:T(1,128)}, u32[]{:S(2)}) copy-start(f32[1,1024]{1,0:T(1,128)} %slice.707) | copy-start | bytes 12292
  289.0 4.3 copy-start
  289.0 3.1 collective-permute-start.4
  294.6 14.9 %collective-permute-start.5 = (bf16[256,1024]{1,0:T(8,128)(2,1)}, bf16[256,1024]{1,0:T(8,128)(2,1)}, u32[]{:S(2)}, u32[]{:S(2)}) collective-permute-start(bf16[256,1024]{1,0:T(8,128)(2,1)} %get-tuple-element.298), channel_id=1, source_target_pairs={{0,1},{1,2},{2,3},{3,0},{4,5},{5,6},{6,7},{7,4},{8,9},{9,10},{10,1... | collective-permute-start | bytes 1572872 | tf_op jit(solution)/shard_map/ppermute | solution.py:62
  294.8 16.6 %collective-permute-start.6 = (bf16[256,1024]{1,0:T(8,128)(2,1)}, bf16[256,1024]{1,0:T(8,128)(2,1)}, u32[]{:S(2)}, u32[]{:S(2)}) collective-permute-start(bf16[256,1024]{1,0:T(8,128)(2,1)} %get-tuple-element.298), channel_id=1, source_target_pairs={{0,3},{1,0},{2,1},{3,2},{4,7},{5,4},{6,5},{7,6},{8,11},{9,8},{10,9... | collective-permute-start | bytes 1572872 | tf_op jit(solution)/shard_map/ppermute | solution.py:67
  309.5 14.0 %collective-permute-start.7 = (bf16[256,1024]{1,0:T(8,128)(2,1)}, bf16[256,1024]{1,0:T(8,128)(2,1)}, u32[]{:S(2)}, u32[]{:S(2)}) collective-permute-start(bf16[256,1024]{1,0:T(8,128)(2,1)} %collective-permute-done.5), channel_id=1, source_target_pairs={{0,1},{1,2},{2,3},{3,0},{4,5},{5,6},{6,7},{7,4},{8,9},{9,10},{10,1... | collective-permute-start | bytes 1572872 | tf_op jit(solution)/shard_map/ppermute | solution.py:62
  325.3 12.3 %copy-start.1 = (f32[256,1024]{1,0:T(8,128)S(1)}, f32[256,1024]{1,0:T(8,128)}, u32[]{:S(2)}) copy-start(f32[256,1024]{1,0:T(8,128)} %copy-done) | copy-start | bytes 3145732
  325.3 12.3 %copy-start.26 = (f32[1,1024]{1,0:T(1,128)S(1)}, f32[1,1024]{1,0:T(1,128)}, u32[]{:S(2)}) copy-start(f32[1,1024]{1,0:T(1,128)} %copy-done.25) | copy-start | bytes 12292
  325.3 12.3 %copy-start.28 = (f32[1,1024]{1,0:T(1,128)S(1)}, f32[1,1024]{1,0:T(1,128)}, u32[]{:S(2)}) copy-start(f32[1,1024]{1,0:T(1,128)} %copy-done.27) | copy-start | bytes 12292
  340.2 4.3 copy-start.5
  352.4 50.3 %copy-start.4 = (f32[256,1024]{1,0:T(8,128)S(1)}, f32[256,1024]{1,0:T(8,128)}, u32[]{:S(2)}) copy-start(f32[256,1024]{1,0:T(8,128)} %get-tuple-element.296) | copy-start | bytes 3145732
  399.9 7.2 %copy-start.29 = (f32[2,1024]{1,0:T(2,128)S(1)}, f32[2,1024]{1,0:T(2,128)}, u32[]{:S(2)}) copy-start(f32[2,1024]{1,0:T(2,128)} %pad_add_fusion) | copy-start | bytes 24580
  399.9 7.3 %copy-start.30 = (f32[2,1024]{1,0:T(2,128)S(1)}, f32[2,1024]{1,0:T(2,128)}, u32[]{:S(2)}) copy-start(f32[2,1024]{1,0:T(2,128)} %pad_add_fusion.1) | copy-start | bytes 24580
  399.9 9.6 %copy-start.18 = (f32[7,1024]{1,0:T(8,128)S(1)}, f32[7,1024]{1,0:T(8,128)}, u32[]{:S(2)}) copy-start(f32[7,1024]{1,0:T(8,128)} %slice.635) | copy-start | bytes 86020
  399.9 9.6 %copy-start.19 = (f32[7,1024]{1,0:T(8,128)S(1)}, f32[7,1024]{1,0:T(8,128)}, u32[]{:S(2)}) copy-start(f32[7,1024]{1,0:T(8,128)} %slice.684) | copy-start | bytes 86020
  401.5 9.5 %copy-start.14 = (f32[15,1024]{1,0:T(8,128)S(1)}, f32[15,1024]{1,0:T(8,128)}, u32[]{:S(2)}) copy-start(f32[15,1024]{1,0:T(8,128)} %slice.631) | copy-start | bytes 184324
  401.6 9.6 %copy-start.15 = (f32[15,1024]{1,0:T(8,128)S(1)}, f32[15,1024]{1,0:T(8,128)}, u32[]{:S(2)}) copy-start(f32[15,1024]{1,0:T(8,128)} %slice.686) | copy-start | bytes 184324
  402.1 5.8 %copy-start.23 = (f32[3,1024]{1,0:T(4,128)S(1)}, f32[3,1024]{1,0:T(4,128)}, u32[]{:S(2)}) copy-start(f32[3,1024]{1,0:T(4,128)} %slice.639) | copy-start | bytes 36868
  402.1 5.8 %copy-start.24 = (f32[3,1024]{1,0:T(4,128)S(1)}, f32[3,1024]{1,0:T(4,128)}, u32[]{:S(2)}) copy-start(f32[3,1024]{1,0:T(4,128)} %slice.682) | copy-start | bytes 36868
  402.7 8.4 %copy-start.43 = (f32[1,1024]{1,0:T(1,128)S(1)}, f32[1,1024]{1,0:T(1,128)}, u32[]{:S(2)}) copy-start(f32[1,1024]{1,0:T(1,128)} %slice.793) | copy-start | bytes 12292
  404.3 7.0 %copy-start.42 = (f32[1,1024]{1,0:T(1,128)S(1)}, f32[1,1024]{1,0:T(1,128)}, u32[]{:S(2)}) copy-start(f32[1,1024]{1,0:T(1,128)} %slice.767) | copy-start | bytes 12292
  408.0 3.4 copy-start.12
  414.4 2.3 copy-start.35
  (9 other events, 8.5 us)
